TPU v7x, 32 devices: a whole 2x2x4 slice. The times are simulated.
32 devices in a mesh: group: 8 (over z, x), member: 4 (over y, core).
Axes of the slice: x: 2, y: 2, z: 4, core: 2. Of those that a mesh axis runs over, the one named last changes fastest.
Arguments:
- prompt_k: bfloat16 [8, 256, 1024], P('group', 'member'), may hold values from -6 to 6
- prompt_v: bfloat16 [8, 256, 1024], P('group', 'member'), may hold values from -18 to 18
- resp_q: bfloat16 [8, 4, 128, 4096], P('group', 'member'), may hold values from -45 to 45
- resp_k: bfloat16 [8, 4, 128, 1024], P('group', 'member'), may hold values from -6 to 6
- resp_v: bfloat16 [8, 4, 128, 1024], P('group', 'member'), may hold values from -18 to 18
- out_grad: bfloat16 [8, 4, 128, 4096], P('group', 'member'), may hold values from -6 to 6
- lengths: int32 [8, 4], P('group', 'member'), may hold values from 16 to 128, as said below
- rewards: float32 [8, 4], P('group', 'member'), may hold values from -6 to 6
Outputs:
- attended: bfloat16 [8, 4, 128, 4096], P('group', 'member')
- grad_q: bfloat16 [8, 4, 128, 4096], P('group', 'member')
- grad_resp_k: bfloat16 [8, 4, 128, 1024], P('group', 'member')
- grad_resp_v: bfloat16 [8, 4, 128, 1024], P('group', 'member')
- grad_prompt_k: bfloat16 [8, 256, 1024], P('group', 'member')
- grad_prompt_v: bfloat16 [8, 256, 1024], P('group', 'member')
Inputs may be any that keep to these rules, and one draw needn't show every extreme that they name: In each group the lengths never fall from one member to the next, and the last member's response has exactly 128 live tokens.
All inputs are finite; a program needn't handle non-finite values.
Results may differ from a plain program's by a relative error of at most 0.0082.
Values may be sent and summed in bfloat16 or wider, within the bound.
A program may use at most 128 MiB of HBM per device.

v0:
```python
import jax
import jax.numpy as jnp
from jax import lax
from jax.sharding import PartitionSpec as P

KVH = 8
HD = 128


def to_heads(rows_in, kv_heads, head_size):
    row_count = rows_in.shape[0]
    per_head = rows_in.shape[1] // (kv_heads * head_size)
    shaped = rows_in.reshape(row_count, kv_heads, per_head, head_size)
    return shaped.transpose(1, 2, 0, 3).reshape(kv_heads, per_head * row_count, head_size)


def from_heads(blocks, row_count):
    kv_heads, rows_all, head_size = blocks.shape
    per_head = rows_all // row_count
    shaped = blocks.reshape(kv_heads, per_head, row_count, head_size)
    return shaped.transpose(2, 0, 1, 3).reshape(row_count, kv_heads * per_head * head_size)


def head_terms(queries, cotangent, all_keys, all_values, allowed, score_scale):
    scores = jnp.dot(queries, all_keys.T, preferred_element_type=jnp.float32) * score_scale
    scores = jnp.where(allowed, scores, -jnp.inf)
    row_max = jnp.max(scores, axis=1, keepdims=True)
    raised = jnp.exp(scores - row_max)
    row_sum = jnp.sum(raised, axis=1, keepdims=True)
    probability = raised / row_sum
    probs_low = probability.astype(jnp.bfloat16)
    output = jnp.dot(probs_low, all_values, preferred_element_type=jnp.float32)
    dprobs = jnp.dot(cotangent, all_values.T, preferred_element_type=jnp.float32)
    row_delta = jnp.sum(cotangent.astype(jnp.float32) * output, axis=1, keepdims=True)
    dscores = (probability * (dprobs - row_delta)).astype(jnp.bfloat16)
    grad_query = jnp.dot(dscores, all_keys, preferred_element_type=jnp.float32) * score_scale
    grad_keys = jnp.dot(dscores.T, queries, preferred_element_type=jnp.float32) * score_scale
    grad_values = jnp.dot(probs_low.T, cotangent, preferred_element_type=jnp.float32)
    return (output, grad_query, grad_keys, grad_values, row_max, row_sum, row_delta)


def body(prompt_k, prompt_v, resp_q, resp_k, resp_v, out_grad, lengths, rewards):
    members = lax.axis_size("member")
    groups = lax.axis_size("group")
    slots = resp_q.shape[2]
    score_scale = float(HD) ** (-0.5)
    length = lengths[0, 0]
    reward = rewards[0, 0]
    own_tokens = length.astype(jnp.float32)
    reward_total = lax.psum(reward, "member")
    token_total = lax.psum(own_tokens, ("group", "member"))
    advantage = reward - reward_total / members
    factor = jnp.float32(slots * groups * members) / token_total
    position = jnp.arange(slots)
    live_rows = position < length
    weight = jnp.where(live_rows, advantage * factor, 0.0)
    cotangent = (out_grad[0, 0].astype(jnp.float32) * weight[:, None]).astype(jnp.bfloat16)
    whole_k, whole_v = (
        lax.all_gather(prompt_k, "member", axis=1, tiled=True),
        lax.all_gather(prompt_v, "member", axis=1, tiled=True),
    )
    prompt_len = whole_k.shape[1]
    all_keys = jnp.concatenate([whole_k[0], resp_k[0, 0]], axis=0)
    all_values = jnp.concatenate([whole_v[0], resp_v[0, 0]], axis=0)
    per_head = resp_q.shape[3] // (KVH * HD)
    row_pos = jnp.tile(position, per_head)
    key_pos = jnp.arange(prompt_len + slots)
    allowed = (key_pos[None, :] < prompt_len) | (key_pos[None, :] - prompt_len <= row_pos[:, None])
    query_heads = to_heads(resp_q[0, 0], KVH, HD)
    cotan_heads = to_heads(cotangent, KVH, HD)
    key_heads = to_heads(all_keys, KVH, HD)
    value_heads = to_heads(all_values, KVH, HD)

    def per_kv_head(head_ops):
        return head_terms(head_ops[0], head_ops[1], head_ops[2], head_ops[3], allowed, score_scale)

    output, grad_query, grad_keys, grad_values, row_max, row_sum, row_delta = lax.map(
        per_kv_head, (query_heads, cotan_heads, key_heads, value_heads)
    )
    attended = (from_heads(output, slots) * live_rows[:, None]).astype(jnp.bfloat16)
    grad_q = from_heads(grad_query, slots).astype(jnp.bfloat16)
    key_rows = from_heads(grad_keys, grad_keys.shape[1])
    value_rows = from_heads(grad_values, grad_values.shape[1])
    grad_resp_k = key_rows[key_rows.shape[0] - slots :].astype(jnp.bfloat16)
    grad_resp_v = value_rows[value_rows.shape[0] - slots :].astype(jnp.bfloat16)
    partial_term = jnp.concatenate([key_rows[:prompt_len], value_rows[:prompt_len]], axis=1)
    summed = lax.psum_scatter(partial_term, "member", scatter_dimension=0, tiled=True)
    row_width = prompt_k.shape[2]
    grad_prompt_k = summed[:, :row_width].astype(jnp.bfloat16)[None]
    grad_prompt_v = summed[:, row_width:].astype(jnp.bfloat16)[None]
    return (
        attended[None, None],
        grad_q[None, None],
        grad_resp_k[None, None],
        grad_resp_v[None, None],
        grad_prompt_k,
        grad_prompt_v,
    )


def solution(mesh):
    placed = (
        P("group", "member", None),
        P("group", "member", None),
        P("group", "member", None, None),
        P("group", "member", None, None),
        P("group", "member", None, None),
        P("group", "member", None, None),
        P("group", "member"),
        P("group", "member"),
    )
    return jax.shard_map(
        body,
        mesh=mesh,
        in_specs=placed,
        out_specs=(
            P("group", "member", None, None),
            P("group", "member", None, None),
            P("group", "member", None, None),
            P("group", "member", None, None),
            P("group", "member", None),
            P("group", "member", None),
        ),
        check_vma=False,
    )
```

profile of v0, /device:TPU:0, one launch (start us, length us, event | category | flops | bytes accessed | tf_op | source)
XLA Modules:
  0.0 201.1 jit_solution(13265405588248452761)
XLA Ops:
  7.9 9.0 %psum.14 = f32[]{:T(128)} all-reduce(f32[]{:T(128)} %bitcast.12), channel_id=1, replica_groups=mesh['group'=8,'member'=4] {'member'}, use_global_device_ids=true, to_apply=%region_0.0 | all-reduce | flops 1 | bytes 8 | tf_op jit(solution)/shard_map/psum | solution.py:50
  17.6 39.6 %psum.15 = f32[]{:T(128)} all-reduce(f32[]{:T(128)S(6)} %convert_element_type.86), channel_id=1, replica_groups=mesh['group'=8,'member'=4] {'group','member'}, use_global_device_ids=true, to_apply=%region_1.0 | all-reduce | flops 1 | bytes 8 | tf_op jit(solution)/shard_map/psum | solution.py:51
  57.2 1.2 copy.74
  58.4 1.8 copy.76
  60.2 8.4 %all_gather.6 = bf16[1,256,1024]{2,1,0:T(8,128)(2,1)S(1)} all-gather(bf16[1,64,1024]{2,1,0:T(8,128)(2,1)} %param.10), channel_id=1, replica_groups=mesh['group'=8,'member'=4] {'member'}, dimensions={1}, use_global_device_ids=true | all-gather | bytes 655360 | tf_op jit(solution)/shard_map/all_gather | solution.py:59
  69.5 7.3 %all_gather.7 = bf16[1,256,1024]{2,1,0:T(8,128)(2,1)S(1)} all-gather(bf16[1,64,1024]{2,1,0:T(8,128)(2,1)S(1)} %copy-done.9), channel_id=1, replica_groups=mesh['group'=8,'member'=4] {'member'}, dimensions={1}, use_global_device_ids=true | all-gather | bytes 655360 | tf_op jit(solution)/shard_map/all_gather | solution.py:60
  78.6 1.4 copy.72
  84.3 1.3 maximum_bitcast_fusion
  85.6 70.0 %while.17 = (s32[]{:T(128)}, f32[8,512,128]{1,2,0:T(8,128)S(1)}, bf16[8,512,128]{2,1,0:T(8,128)(2,1)}, f32[8,384,128]{2,1,0:T(8,128)}, f32[8,384,128]{2,1,0:T(8,...) while((s32[]{:T(128)}, f32[8,512,128]{1,2,0:T(8,128)S(1)}, ...), condition=%wide.region_6.7_spmd.clone, body=%wide.region_2.6_spmd.clone.sunk | while | flops 305838592 | bytes 8159241 | solution.py:77
  85.8 1.3 fusion.63
  90.7 1.9 fusion.66
  92.5 1.8 fusion.67
  94.5 1.3 fusion.63
  97.0 1.2 bitcast_dynamic-update-slice_fusion.2
  98.2 1.2 fusion.65
  99.4 1.9 fusion.66
  101.3 1.8 fusion.67
  103.3 1.3 fusion.63
  108.2 1.9 fusion.66
  110.0 1.9 fusion.67
  112.0 1.3 fusion.63
  114.5 1.2 bitcast_dynamic-update-slice_fusion.2
  116.9 1.9 fusion.66
  118.8 1.8 fusion.67
  120.8 1.3 fusion.63
  123.2 1.2 bitcast_dynamic-update-slice_fusion.2
  125.7 1.9 fusion.66
  127.5 1.9 fusion.67
  129.5 1.3 fusion.63
  134.5 1.9 fusion.66
  136.3 1.9 fusion.67
  138.3 1.3 fusion.63
  140.8 1.2 bitcast_dynamic-update-slice_fusion.2
  142.0 1.2 fusion.65
  143.2 1.9 fusion.66
  145.1 1.8 fusion.67
  147.0 1.3 fusion.63
  149.5 1.2 bitcast_dynamic-update-slice_fusion.2
  150.8 1.2 fusion.65
  152.0 1.9 fusion.66
  153.8 1.8 fusion.67
  155.7 2.1 %slice.41 = f32[256,8,1,128]{3,0,1,2:T(8,128)S(1)} slice(f32[384,8,1,128]{3,0,1,2:T(8,128)} %bitcast.157), slice={[0:256], [0:8], [0:1], [0:128]} | slice | bytes 2097152 | tf_op jit(solution)/shard_map/slice | solution.py:86
  160.0 1.5 pad_maximum_fusion
  166.6 1.6 convert_element_type.93
  168.2 2.1 %reshape.156 = f32[8,4,128,128]{2,1,3,0:T(4,128)S(1)} reshape(f32[8,512,128]{1,2,0:T(8,128)} %copy-done.1) | data formatting | bytes 4194304 | tf_op jit(solution)/shard_map/reshape | solution.py:20
  170.4 2.7 %copy.84 = f32[8,4,128,128]{3,1,0,2:T(4,128)} copy(f32[8,4,128,128]{2,1,3,0:T(4,128)S(1)} %reshape.156) | data formatting | bytes 4194304 | tf_op jit(solution)/shard_map/reshape | solution.py:20
  173.1 2.1 %reshape.157 = f32[1,1,128,4096]{3,2,1,0:T(8,128)S(1)} reshape(f32[128,8,4,128]{3,2,1,0:T(4,128)} %bitcast.146) | data formatting | bytes 4194304 | tf_op jit(solution)/shard_map/reshape | solution.py:21
  176.4 16.1 %reduce-scatter.2.cloned.1.call-done = f32[64,2048]{1,0:T(8,128)} async-done(((f32[256,2048]{1,0:T(8,128)}), f32[64,2048]{1,0:T(8,128)}) %reduce-scatter.2.cloned.1.call-update) | async-done | bytes 524304 | tf_op jit(solution)/shard_map/reduce_scatter | solution.py:87
  (101 shorter events, 36.0 us)
Async XLA Ops:
  7.2 62.4 %copy-start.9 = (bf16[1,64,1024]{2,1,0:T(8,128)(2,1)S(1)}, bf16[1,64,1024]{2,1,0:T(8,128)(2,1)}, u32[]{:S(2)}) copy-start(bf16[1,64,1024]{2,1,0:T(8,128)(2,1)} %param.11) | copy-start | bytes 393220
  7.2 185.3 %reduce-scatter.2.cloned.1.call-start = ((), (), s32[]{:S(2)}) async-start(), calls=%async_computation.1 | async-start | bytes 2621440 | tf_op jit(solution)/shard_map/reduce_scatter | solution.py:87
  57.2 20.7 %copy-start.6 = (bf16[1,1,128,4096]{3,2,1,0:T(8,128)(2,1)S(1)}, bf16[1,1,128,4096]{3,2,1,0:T(8,128)(2,1)}, u32[]{:S(2)}) copy-start(bf16[1,1,128,4096]{3,2,1,0:T(8,128)(2,1)} %param.12) | copy-start | bytes 3145732
  78.6 1.4 copy-start.7
  83.0 1.0 copy-start.2
  83.0 1.2 copy-start.3
  83.0 1.2 copy-start.5
  83.7 1.9 copy-start
  155.7 2.7 %copy-start.1 = (f32[8,512,128]{1,2,0:T(8,128)}, f32[8,512,128]{1,2,0:T(8,128)S(1)}, u32[]{:S(2)}) copy-start(f32[8,512,128]{1,2,0:T(8,128)S(1)} %get-tuple-element.61) | copy-start | bytes 6291460
  157.7 1.4 copy-start.4
  161.5 4.3 %copy-start.8 = (bf16[8,512,128]{2,1,0:T(8,128)(2,1)S(1)}, bf16[8,512,128]{2,1,0:T(8,128)(2,1)}, u32[]{:S(2)}) copy-start(bf16[8,512,128]{2,1,0:T(8,128)(2,1)} %get-tuple-element.62) | copy-start | bytes 3145732
Sparse Core Ops, SparseCore 0:
  161.7 30.7 reduce-scatter.1
where the time goes:
time: 203 us; the launch traced here: 201 us
  matrix products  67.1 us (33%)
  blocking collectives  64.2 us (32%)
  local copies, waits for them, and re-layouts  29.5 us (15%)
  between operations  16.9 us (8%)
  waiting for transfers between devices  16.1 us (8%)
  other arithmetic  7 us (3%)
    psum x1, blocking collectives, body(): token_total = lax.psum(own_tokens, ('group', 'member'))  39.6 us
    reduce_scatter x1, waiting for transfers between devices, body(): lax.psum_scatter(partial_term, 'member', scatter_dimension=0, tiled=True)  16.1 us
    dot_general x8, matrix products, head_terms(): jnp.dot(dscores, all_keys, preferred_element_type=jnp.float32) * score_scale  14.9 us
    dot_general x8, matrix products, head_terms(): jnp.dot(dscores.T, queries, preferred_element_type=jnp.float32)  14.8 us
    dot_general x8, matrix products, head_terms(): jnp.dot(queries, all_keys.T, preferred_element_type=jnp.float32)  10.7 us
    dot_general x8, matrix products, head_terms(): output = jnp.dot(probs_low, all_values, preferred_element_type=jnp.float32)  9.48 us
    dot_general x8, matrix products, head_terms(): jnp.dot(cotangent, all_values.T, preferred_element_type=jnp.float32)  9.48 us
    psum x1, blocking collectives, body(): reward_total = lax.psum(reward, 'member')  9.01 us
  transfers between devices with their start and end apart: 1, of which 1 were waited for; matrix products, arithmetic and copies ran while one was open for 7% of the time, Pallas kernels for 0%

commit v1 on v0

v1 whole, which is shorter than its diff:
```python
import functools

import jax
import jax.numpy as jnp
from jax import lax
from jax.experimental import pallas as pl
from jax.experimental.pallas import tpu as pltpu
from jax.sharding import PartitionSpec as P

KVH = 8
HD = 128
LOG2E = 1.4426950408889634
MESH = pl.DeviceIdType.MESH
NT = (((1,), (1,)), ((), ()))
NN = (((1,), (0,)), ((), ()))
TN = (((0,), (0,)), ((), ()))


def dot(a, b, dims):
    return lax.dot_general(a, b, dims, preferred_element_type=jnp.float32)


def kernel(
    groups, members, rows, slots, per_head,
    length_ref, reward_ref, pk_ref, pv_ref, q_ref, rk_ref, rv_ref, og_ref,
    att_out, gq_out, grk_out, grv_out, gpk_out, gpv_out,
    kall, vall, qbuf, obuf, att, gq, grk, grv, gpk, gpv,
    part, sib_send, sib_recv, x_send, x_recv, stat_send, stat, tok_send, tok, fac,
    in_sem, g_send, f_send, g_recv, s_send, s_recv, t_send, t_recv,
    r_send, r_recv, c_send, c_recv, out_sem, end_sem,
):
    chips = members // 2
    prompt = members * rows
    wide = per_head * slots
    score_scale = float(HD) ** (-0.5)
    group = lax.axis_index("group")
    me = lax.axis_index("member")
    chip = lax.div(me, 2)
    core = lax.rem(me, 2)
    sib = chip * 2 + (1 - core)

    def chip_at(d):
        return lax.rem(chip + d, chips)

    def cols(j, width=HD):
        return pl.ds(pl.multiple_of(j * width, width), width)

    def block_rows(owner):
        return pl.ds(pl.multiple_of(owner * rows, rows), rows)

    def local(src, dst, sem):
        return pltpu.make_async_copy(src, dst, sem)

    def remote(src, dst, send, recv, to_group, to_member):
        return pltpu.make_async_remote_copy(
            src_ref=src, dst_ref=dst, send_sem=send, recv_sem=recv,
            device_id=(to_group, to_member), device_id_type=MESH)

    loads = [
        local(pk_ref.at[0], kall.at[block_rows(me)], in_sem.at[0]),
        local(pv_ref.at[0], vall.at[block_rows(me)], in_sem.at[1]),
        local(rk_ref.at[0, 0], kall.at[pl.ds(prompt, slots)], in_sem.at[2]),
        local(rv_ref.at[0, 0], vall.at[pl.ds(prompt, slots)], in_sem.at[3]),
        local(q_ref.at[0, 0], qbuf, in_sem.at[4]),
        local(og_ref.at[0, 0], obuf, in_sem.at[5]),
    ]
    for load in loads:
        load.start()

    barrier = pltpu.get_barrier_semaphore()
    for step in range(1, members):
        pl.semaphore_signal(barrier, inc=1, device_id=(group, lax.rem(me + step, members)), device_id_type=MESH)
    for step in range(1, groups):
        pl.semaphore_signal(barrier, inc=1, device_id=(lax.rem(group + step, groups), me), device_id_type=MESH)

    length = length_ref[0, 0]
    stat_send[0] = jnp.full((8, HD), length.astype(jnp.float32))
    stat_send[1] = jnp.full((8, HD), reward_ref[0, 0])
    stat[me] = stat_send[...]
    pl.semaphore_wait(barrier, members - 1 + groups - 1)

    sides = ((pk_ref, kall), (pv_ref, vall))

    def direct(side, j, slot):
        to = sib if slot == 0 else chip_at(slot) * 2 + core
        source, whole = sides[side]
        return remote(source.at[0, :, cols(j)], whole.at[block_rows(me), cols(j)],
                      g_send.at[side, j, slot], g_recv.at[side, j, me], group, to)

    def arrival(side, j, owner):
        place = sides[side][1].at[block_rows(owner), cols(j)]
        return remote(place, place, g_send.at[side, j, 0], g_recv.at[side, j, owner], group, sib)

    def forward(side, j, d):
        owner = chip_at(d) * 2 + core
        place = sides[side][1].at[block_rows(owner), cols(j)]
        return remote(place, place, f_send.at[side, j, d - 1], g_recv.at[side, j, owner], group, sib)

    def stat_copy(step):
        return remote(stat_send, stat.at[me], s_send.at[step - 1], s_recv.at[me], group, lax.rem(me + step, members))

    def tok_copy(step):
        return remote(tok_send, tok.at[group], t_send.at[step - 1], t_recv.at[group],
                      lax.rem(group + step, groups), me)

    def send_head(j, carry):
        for slot in list(range(1, chips)) + [0]:
            for side in range(2):
                direct(side, j, slot).start()
        return carry

    send_head(0, 0)
    for step in range(1, members):
        stat_copy(step).start()
    lax.fori_loop(1, KVH, send_head, 0)

    for step in range(1, members):
        owner = lax.rem(me + step, members)
        remote(stat_send, stat.at[owner], s_send.at[0], s_recv.at[owner], group, owner).wait_recv()
    tok_send[...] = functools.reduce(jnp.add, [stat[i, 0] for i in range(members)])
    tok[group] = tok_send[...]
    for step in range(1, groups):
        tok_copy(step).start()
    reward_total = functools.reduce(jnp.add, [stat[i, 1] for i in range(members)])
    advantage = stat_send[1] - reward_total / members
    adv_row = advantage[0:1]

    def forward_head(j):
        for d in range(1, chips):
            owner = chip_at(d) * 2 + core
            for side in range(2):
                arrival(side, j, owner).wait_recv()
                forward(side, j, d).start()

    forward_head(0)
    for load in loads:
        load.wait()

    u_pos = lax.broadcasted_iota(jnp.int32, (slots, wide), 0)
    t_pos = lax.rem(lax.broadcasted_iota(jnp.int32, (slots, wide), 1), slots)
    causal = u_pos <= t_pos
    live_lane = lax.rem(lax.broadcasted_iota(jnp.int32, (HD, wide), 1), slots) < length
    live_row = lax.rem(lax.broadcasted_iota(jnp.int32, (wide, HD), 0), slots) < length

    def sib_copy(j):
        return remote(sib_send.at[j], sib_recv.at[j], r_send.at[j], r_recv.at[j], group, sib)

    def cross_copy(j, d):
        return remote(x_send.at[j, d - 1], x_recv.at[j, d - 1], c_send.at[j, d - 1], c_recv.at[j, d - 1],
                      group, chip_at(d) * 2 + core)

    def cross_head(j):
        sib_copy(j).wait_recv()
        for d in range(1, chips):
            own = part[j, chip_at(d) * 2 + core]
            x_send[j, d - 1] = (own + sib_recv[j, d].astype(jnp.float32)).astype(jnp.bfloat16)
            cross_copy(j, d).start()

    def out_copies(j):
        return [
            local(att.at[:, cols(j, per_head * HD)], att_out.at[0, 0, :, cols(j, per_head * HD)], out_sem.at[0, j]),
            local(gq.at[:, cols(j, per_head * HD)], gq_out.at[0, 0, :, cols(j, per_head * HD)], out_sem.at[1, j]),
            local(grk.at[:, cols(j)], grk_out.at[0, 0, :, cols(j)], out_sem.at[2, j]),
            local(grv.at[:, cols(j)], grv_out.at[0, 0, :, cols(j)], out_sem.at[3, j]),
        ]

    def head(j, carry):
        @pl.when(j + 1 < KVH)
        def _():
            forward_head(j + 1)

        for side in range(2):
            arrival(side, j, sib).wait_recv()
            for d in range(1, chips):
                arrival(side, j, chip_at(d) * 2 + (1 - core)).wait_recv()

        k = kall[:, cols(j)]
        v = vall[:, cols(j)]
        qs = [qbuf[:, cols(j * per_head + h)] for h in range(per_head)]
        gs = [obuf[:, cols(j * per_head + h)] for h in range(per_head)]
        q = jnp.concatenate(qs, axis=0)
        g = jnp.concatenate(gs, axis=0)
        g = jnp.where(live_row, g, jnp.zeros_like(g))
        s = dot(k, q, NT)
        s = jnp.concatenate([s[:prompt], jnp.where(causal, s[prompt:], -1e30)], axis=0)
        top = jnp.max(s, axis=0, keepdims=True)
        e = jnp.exp2((s - top) * (score_scale * LOG2E))
        p = e * (1.0 / jnp.sum(e, axis=0, keepdims=True))
        p_low = p.astype(jnp.bfloat16)
        dp = dot(v, g, NT)
        delta = jnp.sum(p * dp, axis=0, keepdims=True)
        ds = (p * (dp - delta)).astype(jnp.bfloat16)
        dk = dot(ds, q, NN) * (adv_row * score_scale)
        dv = dot(p_low, g, NN) * adv_row
        part[j, :, :, :HD] = dk[:prompt].reshape(members, rows, HD)
        part[j, :, :, HD:] = dv[:prompt].reshape(members, rows, HD)
        for d in range(chips):
            sib_send[j, d] = part[j, chip_at(d) * 2 + (1 - core)].astype(jnp.bfloat16)
        sib_copy(j).start()

        @pl.when(j == 0)
        def _():
            for step in range(1, groups):
                owner = lax.rem(group + step, groups)
                remote(tok_send, tok.at[owner], t_send.at[0], t_recv.at[owner], owner, me).wait_recv()
            total = functools.reduce(jnp.add, [tok[i] for i in range(groups)])
            fac[...] = float(slots * groups * members) / total

        factor = fac[0:1]
        grk[:, cols(j)] = (dk[prompt:] * factor).astype(jnp.bfloat16)
        grv[:, cols(j)] = (dv[prompt:] * factor).astype(jnp.bfloat16)
        o_t = dot(v, p_low, TN)
        o_t = jnp.where(live_lane, o_t, 0.0).astype(jnp.bfloat16)
        dq_t = dot(k, ds, TN)
        weight = (adv_row * factor) * score_scale
        dq_t = (dq_t * weight[0:1, 0:1]).astype(jnp.bfloat16)
        for h in range(per_head):
            att[:, cols(j * per_head + h)] = o_t[:, h * slots:(h + 1) * slots].T
            gq[:, cols(j * per_head + h)] = dq_t[:, h * slots:(h + 1) * slots].T
        for copy in out_copies(j):
            copy.start()

        @pl.when(j > 0)
        def _():
            cross_head(j - 1)

        return carry

    lax.fori_loop(0, KVH, head, 0)
    cross_head(KVH - 1)

    def finish(j, carry):
        total = part[j, me] + sib_recv[j, 0].astype(jnp.float32)
        for d in range(1, chips):
            cross_copy(j, d).wait_recv()
            total = total + x_recv[j, d - 1].astype(jnp.float32)
        factor = fac[0:1]
        gpk[:, cols(j)] = (total[:, :HD] * factor).astype(jnp.bfloat16)
        gpv[:, cols(j)] = (total[:, HD:] * factor).astype(jnp.bfloat16)
        return carry

    lax.fori_loop(0, KVH, finish, 0)
    ends = [local(gpk, gpk_out.at[0], end_sem.at[0]), local(gpv, gpv_out.at[0], end_sem.at[1])]
    for copy in ends:
        copy.start()

    def drain(j, carry):
        for side in range(2):
            for slot in range(chips):
                direct(side, j, slot).wait_send()
            for d in range(1, chips):
                forward(side, j, d).wait_send()
        sib_copy(j).wait_send()
        for d in range(1, chips):
            cross_copy(j, d).wait_send()
        for copy in out_copies(j):
            copy.wait()
        return carry

    lax.fori_loop(0, KVH, drain, 0)
    for step in range(1, members):
        stat_copy(step).wait_send()
    for step in range(1, groups):
        tok_copy(step).wait_send()
    for copy in ends:
        copy.wait()


def body(prompt_k, prompt_v, resp_q, resp_k, resp_v, out_grad, lengths, rewards):
    members = lax.axis_size("member")
    groups = lax.axis_size("group")
    chips = members // 2
    rows = prompt_k.shape[1]
    slots = resp_q.shape[2]
    per_head = resp_q.shape[3] // (KVH * HD)
    keys = members * rows + slots
    width = KVH * HD
    bf, f32 = jnp.bfloat16, jnp.float32
    dma = pltpu.SemaphoreType.DMA
    crossing = max(chips - 1, 1)
    scratch = [
        pltpu.VMEM((keys, width), bf),
        pltpu.VMEM((keys, width), bf),
        pltpu.VMEM((slots, width * per_head), bf),
        pltpu.VMEM((slots, width * per_head), bf),
        pltpu.VMEM((slots, width * per_head), bf),
        pltpu.VMEM((slots, width * per_head), bf),
        pltpu.VMEM((slots, width), bf),
        pltpu.VMEM((slots, width), bf),
        pltpu.VMEM((rows, width), bf),
        pltpu.VMEM((rows, width), bf),
        pltpu.VMEM((KVH, members, rows, 2 * HD), f32),
        pltpu.VMEM((KVH, chips, rows, 2 * HD), bf),
        pltpu.VMEM((KVH, chips, rows, 2 * HD), bf),
        pltpu.VMEM((KVH, crossing, rows, 2 * HD), bf),
        pltpu.VMEM((KVH, crossing, rows, 2 * HD), bf),
        pltpu.VMEM((2, 8, HD), f32),
        pltpu.VMEM((members, 2, 8, HD), f32),
        pltpu.VMEM((8, HD), f32),
        pltpu.VMEM((groups, 8, HD), f32),
        pltpu.VMEM((8, HD), f32),
        dma((6,)),
        dma((2, KVH, chips)),
        dma((2, KVH, crossing)),
        dma((2, KVH, members)),
        dma((members,)),
        dma((members,)),
        dma((groups,)),
        dma((groups,)),
        dma((KVH,)),
        dma((KVH,)),
        dma((KVH, crossing)),
        dma((KVH, crossing)),
        dma((4, KVH)),
        dma((2,)),
    ]
    held = pl.BlockSpec(memory_space=pl.ANY)
    scalar = pl.BlockSpec(memory_space=pltpu.SMEM)
    flops = 10 * slots * width * per_head * keys
    moved = sum(2 * a.size * a.dtype.itemsize for a in (resp_q, out_grad, resp_k, resp_v, prompt_k, prompt_v))
    return pl.pallas_call(
        functools.partial(kernel, groups, members, rows, slots, per_head),
        out_shape=[
            jax.ShapeDtypeStruct(a.shape, bf) for a in (resp_q, resp_q, resp_k, resp_v, prompt_k, prompt_v)
        ],
        in_specs=[scalar, scalar] + [held] * 6,
        out_specs=[held] * 6,
        scratch_shapes=scratch,
        compiler_params=pltpu.CompilerParams(
            collective_id=0, has_side_effects=True, vmem_limit_bytes=48 * 1024 * 1024),
        cost_estimate=pl.CostEstimate(
            flops=flops, bytes_accessed=moved, transcendentals=slots * KVH * per_head * keys),
        name="shared_prompt_attention",
    )(lengths, rewards, prompt_k, prompt_v, resp_q, resp_k, resp_v, out_grad)


def solution(mesh):
    rows = P("group", "member", None)
    wide = P("group", "member", None, None)
    return jax.shard_map(
        body,
        mesh=mesh,
        in_specs=(rows, rows, wide, wide, wide, wide, P("group", "member"), P("group", "member")),
        out_specs=(wide, wide, wide, wide, rows, rows),
        check_vma=False,
    )
```

time: 203 us -> 43.1 us (0.21)
  matrix products: 67.1 us -> 0 us
  blocking collectives: 64.2 us -> 0 us
  Pallas kernels: 0 us -> 30 us
  local copies, waits for them, and re-layouts: 29.5 us -> 10.8 us
  waiting for transfers between devices: 16.1 us -> 0 us
  between operations: 16.9 us -> 1.95 us
  other arithmetic: 7 us -> 0 us
    dot_general x48 -> x0, matrix products: 67.1 us -> none  [the longest x8 14.9 us: head_terms(): jnp.dot(dscores, all_keys, preferred_element_type=jnp.float32) * score_scale]
    psum x2 -> x0, blocking collectives: 48.6 us -> none  [the longest x1 39.6 us: body(): token_total = lax.psum(own_tokens, ('group', 'member'))]
    pallas_call x0 -> x1, Pallas kernels: none -> 30 us  [body(): pl.pallas_call(functools.partial(kernel, groups, members, rows, slots, pe...]
    reduce_scatter x1 -> x0, waiting for transfers between devices: 16.1 us -> none  [body(): lax.psum_scatter(partial_term, 'member', scatter_dimension=0, tiled=True)]
    all_gather x2 -> x0, blocking collectives: 15.6 us -> none  [the longest x1 8.35 us: body(): lax.all_gather(prompt_k, 'member', axis=1, tiled=True)]
    reshape x3 -> x0, local copies, waits for them, and re-layouts: 6.93 us -> none  [the longest x2 4.82 us: from_heads(): shaped = blocks.reshape(kv_heads, per_head, row_count, head_size)]
    slice x8 -> x0, local copies, waits for them, and re-layouts: 5.95 us -> none  [the longest x2 2.66 us: body(): value_rows[:prompt_len]]
    unnamed x25 -> x18, local copies, waits for them, and re-layouts: 5.22 us -> 10.8 us
  transfers between devices with their start and end apart: 1 -> 0, of which waited for: 1 -> 0; matrix products, arithmetic and copies ran while one was open for 7% -> 0% of each run, Pallas kernels for 0% -> 0%
where the time goes in v1:
time: 43.1 us; the launch traced here: 42.8 us
  Pallas kernels  30 us (70%)
  local copies, waits for them, and re-layouts  10.8 us (25%)
  between operations  1.95 us (5%)
    pallas_call x1, Pallas kernels, body(): pl.pallas_call(functools.partial(kernel, groups, members, rows, slots, pe...  30 us
    unnamed x18, local copies, waits for them, and re-layouts  10.8 us

profile of v1, /device:TPU:0, one launch (start us, length us, event | category | flops | bytes accessed | tf_op | source)
XLA Modules:
  0.0 42.8 jit_solution(11701925411014587892)
XLA Ops:
  1.9 0.0 copy-start
  1.9 1.2 %copy-done = bf16[1,1,128,4096]{3,2,1,0:T(8,128)(2,1)S(1)} copy-done((bf16[1,1,128,4096]{3,2,1,0:T(8,128)(2,1)S(1)}, bf16[1,1,128,4096]{3,2,1,0:T(8,128)(2,1)}, u32[]{:S(2)}) %copy-start) | copy-done | bytes 1048600
  3.2 0.0 copy-start.1
  3.2 1.2 %copy-done.1 = bf16[1,1,128,4096]{3,2,1,0:T(8,128)(2,1)S(1)} copy-done((bf16[1,1,128,4096]{3,2,1,0:T(8,128)(2,1)S(1)}, bf16[1,1,128,4096]{3,2,1,0:T(8,128)(2,1)}, u32[]{:S(2)}) %copy-start.1) | copy-done | bytes 1048600
  4.4 0.0 copy-start.2
  4.4 0.9 %copy-done.2 = bf16[1,1,128,1024]{3,2,1,0:T(8,128)(2,1)S(1)} copy-done((bf16[1,1,128,1024]{3,2,1,0:T(8,128)(2,1)S(1)}, bf16[1,1,128,1024]{3,2,1,0:T(8,128)(2,1)}, u32[]{:S(2)}) %copy-start.2) | copy-done | bytes 262168
  5.3 0.0 copy-start.3
  5.3 0.9 %copy-done.3 = bf16[1,1,128,1024]{3,2,1,0:T(8,128)(2,1)S(1)} copy-done((bf16[1,1,128,1024]{3,2,1,0:T(8,128)(2,1)S(1)}, bf16[1,1,128,1024]{3,2,1,0:T(8,128)(2,1)}, u32[]{:S(2)}) %copy-start.3) | copy-done | bytes 262168
  6.3 0.0 copy-start.4
  6.3 0.9 %copy-done.4 = bf16[1,64,1024]{2,1,0:T(8,128)(2,1)S(1)} copy-done((bf16[1,64,1024]{2,1,0:T(8,128)(2,1)S(1)}, bf16[1,64,1024]{2,1,0:T(8,128)(2,1)}, u32[]{:S(2)}) %copy-start.4) | copy-done | bytes 131096
  7.2 0.0 copy-start.5
  7.2 0.9 %copy-done.5 = bf16[1,64,1024]{2,1,0:T(8,128)(2,1)S(1)} copy-done((bf16[1,64,1024]{2,1,0:T(8,128)(2,1)S(1)}, bf16[1,64,1024]{2,1,0:T(8,128)(2,1)}, u32[]{:S(2)}) %copy-start.5) | copy-done | bytes 131096
  8.1 30.0 %shared_prompt_attention.1 = (bf16[1,1,128,4096]{3,2,1,0:T(8,128)(2,1)S(1)}, bf16[1,1,128,4096]{3,2,1,0:T(8,128)(2,1)S(1)}, bf16[1,1,128,1024]{3,2,1,0:T(8,128)(...) custom-call(s32[1,1]{1,0:T(1,128)S(6)} %copy.20.length_ref, ...), custom_call_target="tpu_custom_call" | custom-call | flops 2013265920 | bytes 5767168 | tf_op jit(solution)/shard_map/shared_prompt_attention/pallas_call | solution.py:321
  38.1 1.0 %copy.22 = bf16[1,1,128,4096]{3,2,1,0:T(8,128)(2,1)} copy(bf16[1,1,128,4096]{3,2,1,0:T(8,128)(2,1)S(1)} %get-tuple-element.12) | data formatting | bytes 2097152
  39.1 1.0 %copy.23 = bf16[1,1,128,4096]{3,2,1,0:T(8,128)(2,1)} copy(bf16[1,1,128,4096]{3,2,1,0:T(8,128)(2,1)S(1)} %get-tuple-element.13) | data formatting | bytes 2097152
  40.1 0.7 %copy.24 = bf16[1,1,128,1024]{3,2,1,0:T(8,128)(2,1)} copy(bf16[1,1,128,1024]{3,2,1,0:T(8,128)(2,1)S(1)} %get-tuple-element.14) | data formatting | bytes 524288
  40.8 0.7 %copy.25 = bf16[1,1,128,1024]{3,2,1,0:T(8,128)(2,1)} copy(bf16[1,1,128,1024]{3,2,1,0:T(8,128)(2,1)S(1)} %get-tuple-element.15) | data formatting | bytes 524288
  41.5 0.7 %copy.26 = bf16[1,64,1024]{2,1,0:T(8,128)(2,1)} copy(bf16[1,64,1024]{2,1,0:T(8,128)(2,1)S(1)} %get-tuple-element.16) | data formatting | bytes 262144
  42.1 0.7 %copy.27 = bf16[1,64,1024]{2,1,0:T(8,128)(2,1)} copy(bf16[1,64,1024]{2,1,0:T(8,128)(2,1)S(1)} %get-tuple-element.17) | data formatting | bytes 262144
Async XLA Ops:
  1.9 1.2 %copy-start = (bf16[1,1,128,4096]{3,2,1,0:T(8,128)(2,1)S(1)}, bf16[1,1,128,4096]{3,2,1,0:T(8,128)(2,1)}, u32[]{:S(2)}) copy-start(bf16[1,1,128,4096]{3,2,1,0:T(8,128)(2,1)} %q_ref.1) | copy-start | bytes 3145732
  3.2 1.2 %copy-start.1 = (bf16[1,1,128,4096]{3,2,1,0:T(8,128)(2,1)S(1)}, bf16[1,1,128,4096]{3,2,1,0:T(8,128)(2,1)}, u32[]{:S(2)}) copy-start(bf16[1,1,128,4096]{3,2,1,0:T(8,128)(2,1)} %og_ref.1) | copy-start | bytes 3145732
  4.4 0.9 %copy-start.2 = (bf16[1,1,128,1024]{3,2,1,0:T(8,128)(2,1)S(1)}, bf16[1,1,128,1024]{3,2,1,0:T(8,128)(2,1)}, u32[]{:S(2)}) copy-start(bf16[1,1,128,1024]{3,2,1,0:T(8,128)(2,1)} %rk_ref.1) | copy-start | bytes 786436
  5.3 0.9 %copy-start.3 = (bf16[1,1,128,1024]{3,2,1,0:T(8,128)(2,1)S(1)}, bf16[1,1,128,1024]{3,2,1,0:T(8,128)(2,1)}, u32[]{:S(2)}) copy-start(bf16[1,1,128,1024]{3,2,1,0:T(8,128)(2,1)} %rv_ref.1) | copy-start | bytes 786436
  6.3 0.9 %copy-start.4 = (bf16[1,64,1024]{2,1,0:T(8,128)(2,1)S(1)}, bf16[1,64,1024]{2,1,0:T(8,128)(2,1)}, u32[]{:S(2)}) copy-start(bf16[1,64,1024]{2,1,0:T(8,128)(2,1)} %pk_ref.1) | copy-start | bytes 393220
  7.2 0.9 %copy-start.5 = (bf16[1,64,1024]{2,1,0:T(8,128)(2,1)S(1)}, bf16[1,64,1024]{2,1,0:T(8,128)(2,1)}, u32[]{:S(2)}) copy-start(bf16[1,64,1024]{2,1,0:T(8,128)(2,1)} %pv_ref.1) | copy-start | bytes 393220
